TPU v7x, 32 devices: a whole 2x2x4 slice. The times are simulated.
32 devices in a mesh: groups: 1, blk: 32 (over z, y, x, core), term: 1.
Axes of the slice: x: 2, y: 2, z: 4, core: 2. Of those that a mesh axis runs over, the one named last changes fastest.
Arguments:
- wavefunction: bfloat16 [1792, 128, 128], P(('groups', 'blk')), may hold values from -6 to 6
- left_environment: bfloat16 [224, 2, 128, 128], P(('groups', 'blk'), 'term'), may hold values from -0.5 to 0.5
- right_environment: bfloat16 [224, 2, 128, 128], P(('groups', 'blk'), 'term'), may hold values from -0.5 to 0.5
- right_sector: int32 [1792], P(('groups', 'blk')), may hold values from 0 to 223, as said below
- left_dims: int32 [224], P(('groups', 'blk')), may hold values from 32 to 128, as said below
- right_dims: int32 [224], P(('groups', 'blk')), may hold values from 32 to 128, as said below
Outputs:
- product_blocks: bfloat16 [1792, 128, 128], P(('groups', 'blk'), 'term')
Inputs may be any that keep to these rules, and one draw needn't show every extreme that they name: `right_sector`: block k lies on blk index floor(k / 56); the sectors s with equal floor(s / 7) form an aligned run. At most 3 blocks of one blk index name sectors of one run, and in every draw one run is named by exactly 3 blocks of every blk index. `left_dims`: some sector has dimension exactly 128. `right_dims`: some sector has dimension exactly 128.
All inputs are finite; a program needn't handle non-finite values.
Results may differ from a plain program's by a relative error of at most 0.0059.
Values may be sent and summed in bfloat16 or wider, within the bound.
A program may use at most 128 MiB of HBM per device.

v0:
```python
import jax
import jax.numpy as jnp
from jax import lax
from jax.sharding import PartitionSpec as P

PER_SECTOR = 8


def keep_below(limits, extent):
    return jnp.arange(extent, dtype=jnp.int32)[None, :] < limits[:, None]


def body(wavefunction, left_environment, right_environment, right_sector, left_dims, right_dims):
    devices = lax.axis_size("blk")
    blocks_here, extent, _ = wavefunction.shape
    sectors_here, terms_here = (left_environment.shape[0], left_environment.shape[1])
    capacity = max(1, 2 * blocks_here // devices)
    slots_all = devices * capacity
    left_index = jnp.arange(blocks_here, dtype=jnp.int32) // PER_SECTOR
    row_keep = keep_below(left_dims[left_index], extent)
    masked = jnp.where(row_keep[:, :, None], wavefunction, jnp.zeros((), jnp.bfloat16))
    grouped = masked.reshape(sectors_here, PER_SECTOR, extent, extent)
    left_part = jnp.einsum(
        "atij,apjk->aptik", left_environment, grouped, preferred_element_type=jnp.float32
    )
    left_part = left_part.astype(jnp.bfloat16).reshape(blocks_here, terms_here, extent, extent)
    holder = right_sector // sectors_here
    local_sector = right_sector % sectors_here
    block_numbers = jnp.arange(blocks_here, dtype=jnp.int32)
    same_holder = holder[:, None] == holder[None, :]
    earlier = block_numbers[None, :] < block_numbers[:, None]
    position = jnp.sum(same_holder & earlier, axis=1)
    slot_index = holder * capacity + position
    matches = slot_index[None, :] == jnp.arange(slots_all, dtype=jnp.int32)[:, None]
    filled = jnp.any(matches, axis=1)
    source = jnp.sum(jnp.where(matches, block_numbers[None, :], 0), axis=1)
    source = jnp.where(filled, source, blocks_here)
    wanted = jnp.where(filled, local_sector[jnp.minimum(source, blocks_here - 1)], -1)
    wanted = wanted.reshape(devices, capacity)
    padded = jnp.concatenate(
        [left_part, jnp.zeros((1, terms_here, extent, extent), jnp.bfloat16)], axis=0
    )
    outgoing = jnp.take(padded, source, axis=0).reshape(
        devices, capacity, terms_here, extent, extent
    )
    arrived = lax.all_to_all(outgoing, "blk", split_axis=0, concat_axis=0, tiled=True)
    labels = lax.all_to_all(wanted, "blk", split_axis=0, concat_axis=0, tiled=True)
    senders, per_sender = labels.shape
    flat_labels = labels.reshape(senders * per_sender)
    clipped = jnp.clip(flat_labels, 0, sectors_here - 1)
    limits = jnp.where(flat_labels >= 0, right_dims[clipped], 0)
    col_keep = keep_below(limits, extent)
    flattened = arrived.reshape(senders * per_sender, terms_here, extent, extent)
    flattened = jnp.where(col_keep[:, None, None, :], flattened, jnp.zeros((), jnp.bfloat16))
    operators = right_environment[clipped]
    products = jnp.einsum(
        "ntij,ntjk->nik", flattened, operators, preferred_element_type=jnp.float32
    )
    products = jnp.where(col_keep[:, None, :], products, 0.0).astype(jnp.bfloat16)
    returned = lax.all_to_all(
        products.reshape(senders, per_sender, extent, extent),
        "blk",
        split_axis=0,
        concat_axis=0,
        tiled=True,
    )
    partial_value = returned.reshape(slots_all, extent, extent)[slot_index]
    summed = lax.psum_scatter(
        partial_value.astype(jnp.float32).astype(jnp.bfloat16),
        "term",
        scatter_dimension=1,
        tiled=True,
    ).astype(jnp.float32)
    rows_here = summed.shape[1]
    row_numbers = lax.axis_index("term") * rows_here + jnp.arange(rows_here, dtype=jnp.int32)
    keep_rows = row_numbers[None, :] < left_dims[left_index][:, None]
    return jnp.where(keep_rows[:, :, None], summed, 0.0).astype(jnp.bfloat16)


def solution(mesh):
    placed = (
        P(("groups", "blk"), None, None),
        P(("groups", "blk"), "term", None, None),
        P(("groups", "blk"), "term", None, None),
        P(("groups", "blk")),
        P(("groups", "blk")),
        P(("groups", "blk")),
    )
    return jax.shard_map(
        body,
        mesh=mesh,
        in_specs=placed,
        out_specs=P(("groups", "blk"), "term", None),
        check_vma=False,
    )
```

profile of v0, /device:TPU:1, one launch (start us, length us, event | category | flops | bytes accessed | tf_op | source)
XLA Modules:
  0.0 279.2 jit_solution(5380825482637052110)
XLA Ops:
  0.0 0.0 copy-start
  0.0 0.0 copy-start.2
  0.0 0.8 and_select_fusion
  0.8 0.2 convert_reduce_fusion
  0.9 0.1 fusion.2
  1.0 0.1 select_reduce_fusion
  1.2 1.2 gather_fusion
  2.4 0.7 select_n.153
  3.1 7.1 %all-to-all-start = ((s32[32,1,3]{2,1,0:T(1,128)}), s32[32,1,3]{2,1,0:T(1,128)S(1)}, u32[]{:S(2)}, u32[]{:S(2)}) async-start(s32[32,1,3]{2,1,0:T(1,128)} %bitcast.10), calls=%async_computation | async-start | bytes 32768 | tf_op jit(solution)/shard_map/all_to_all | solution.py:47
  10.2 0.1 select_n.156
  10.3 1.6 fusion.9
  11.9 4.3 %fusion.5 = s32[56]{0:T(128)S(1)} fusion(s32[]{:T(128)} %bitcast, s32[]{:T(128)} %bitcast.1, s32[]{:T(128)} %bitcast.2, s32[]{:T(128)} %bitcast.3, s32[]{:T(128)} %bitcast.4, s32[]{:T(128)} %bitcast.6, s32[]{:T(128)} %bitcast.5), kind=kLoop, calls=%fused_computation.52 | loop fusion | flops 1288 | bytes 252 | tf_op jit(solution)/shard_map/gather | solution.py:76
  16.3 0.1 iota_compare_fusion.3
  16.3 3.0 %broadcast_select_fusion.1 = bf16[56,128,128]{2,1,0:T(8,128)(2,1)S(1)} fusion(bf16[56,128,128]{2,1,0:T(8,128)(2,1)} %param.6, pred[56,128]{1,0:T(8,128)(4,1)S(1)} %iota_compare_fusion.3), kind=kLoop, calls=%fused_computation.10 | loop fusion | flops 917504 | bytes 3677184 | tf_op jit(solution)/shard_map/jit(_where)/select_n | solution.py:21
  19.4 0.0 copy-done.2
  19.4 1.2 convolution_convert_fusion
  20.6 2.2 concatenate.3
  22.7 8.0 %gather_fusion.1 = bf16[96,2,128,128]{2,3,1,0:T(8,128)(2,1)} fusion(bf16[57,2,128,128]{2,3,1,0:T(8,128)(2,1)} %concatenate.3, s32[1024]{0:T(1024)S(1)} %pad_clamp_fusion.2), kind=kCustom, calls=%fused_computation.1 | custom fusion | bytes 12583296 | tf_op jit(solution)/shard_map/jit(_take)/gather | solution.py:43
  30.7 8.7 %copy.16 = bf16[32,3,2,128,128]{4,3,2,1,0:T(8,128)(2,1)} copy(bf16[32,3,2,128,128]{3,4,2,1,0:T(8,128)(2,1)} %bitcast.56) | data formatting | bytes 12582912 | tf_op jit(solution)/shard_map/jit(_take)/gather | solution.py:43
  39.4 6.0 %broadcast_select_fusion = bf16[32,3,2,128,128]{4,3,2,1,0:T(8,128)(2,1)} fusion(bf16[32,3,2,128,128]{4,3,2,1,0:T(8,128)(2,1)} %copy.16, pred[32,3]{1,0:T(8,128)(4,1)S(1)} %compare_and_fusion), kind=kLoop, calls=%fused_computation.7 | loop fusion | flops 3145728 | bytes 12583008 | tf_op jit(solution)/shard_map/jit(_take)/select_n | solution.py:43
  45.4 0.0 copy-start.3
  45.4 0.0 all-to-all-done
  45.4 5.9 %all-to-all-start.1 = ((bf16[32,3,2,128,128]{4,3,2,1,0:T(8,128)(2,1)}), bf16[32,3,2,128,128]{4,3,2,1,0:T(8,128)(2,1)}, u32[]{:S(2)}, u32[]{:S(2)}) async-start(bf16[32,3,2,128,128]{4,3,2,1,0:T(8,128)(2,1)} %broadcast_select_fusion), calls=%async_computation.1 | async-start | bytes 12582912 | tf_op jit(solution)/shard_map/all_to_all | solution.py:46
  51.3 0.0 copy-done.3
  51.3 0.7 fusion.10
  52.0 0.1 clamp_reduce_fusion
  52.0 0.1 min.27
  52.1 0.1 compare_reduce_fusion
  52.2 0.1 ge.21
  52.3 0.0 copy-done
  52.4 5.9 %gather_fusion.2 = bf16[96,2,128,128]{3,2,1,0:T(8,128)(2,1)} fusion(bf16[7,2,128,128]{3,2,1,0:T(8,128)(2,1)S(1)} %copy-done, s32[1024]{0:T(1024)S(1)} %pad_clamp_fusion.1), kind=kCustom, calls=%fused_computation.2 | custom fusion | bytes 12583296 | tf_op jit(solution)/shard_map/gather | solution.py:55
  58.3 4.4 %fusion.4 = s32[96]{0:T(128)S(1)} fusion(pred[96]{0:T(512)(128)(4,1)S(1)} %ge.21, s32[]{:T(128)} %bitcast.12, s32[]{:T(128)} %bitcast.13, s32[]{:T(128)} %bitcast.14, s32[]{:T(128)} %bitcast.15, s32[]{:T(128)} %bitcast.16, s32[]{:T(128)} %bitcast.17, s32[]{:T(128)} %bitcast.18, s32[96,1]{0,1:T(1,128)S(1)} %min.27), kind=kLoop, calls=%fused_computation.51 | loop fusion | flops 1536 | bytes 892 | tf_op jit(solution)/shard_map/jit(_where)/select_n | solution.py:51
  62.7 0.1 iota_compare_fusion
  62.7 128.0 %all-to-all-done.1 = bf16[32,3,2,128,128]{4,3,2,1,0:T(8,128)(2,1)} async-done(((bf16[32,3,2,128,128]{4,3,2,1,0:T(8,128)(2,1)}), bf16[32,3,2,128,128]{4,3,2,1,0:T(8,128)(2,1)}, u32[]{:S(2)}, u32[]{:S(2)}) %all-to-all-start.1) | async-done | bytes 6291488 | tf_op jit(solution)/shard_map/all_to_all | solution.py:46
  190.8 0.0 copy-start.1
  190.8 3.4 %bitcast_select_fusion.1 = bf16[96,2,128,128]{3,2,1,0:T(8,128)(2,1)S(1)} fusion(bf16[32,3,2,128,128]{4,3,2,1,0:T(8,128)(2,1)} %all-to-all-done.1, pred[96,128]{1,0:T(8,128)(4,1)S(1)} %iota_compare_fusion), kind=kLoop, calls=%fused_computation.6 | loop fusion | flops 3145728 | bytes 12595200 | tf_op jit(solution)/shard_map/jit(_where)/select_n | solution.py:54
  194.2 1.2 copy-done.1
  195.4 3.5 %fusion = bf16[96,128,128]{2,1,0:T(8,128)(2,1)} fusion(pred[96,128]{1,0:T(8,128)(4,1)S(1)} %iota_compare_fusion, bf16[96,2,128,128]{3,2,1,0:T(8,128)(2,1)S(1)} %bitcast_select_fusion.1, bf16[96,2,128,128]{3,2,1,0:T(8,128)(2,1)S(1)} %copy-done.1), kind=kOutput, calls=%fused_computation.5 | convolution fusion | flops 808452096 | bytes 15740928 | tf_op jit(solution)/shard_map/ntij,ntjk->nik/dot_general | solution.py:56
  198.9 3.9 %all-to-all-start.2 = ((bf16[32,3,128,128]{3,2,1,0:T(8,128)(2,1)}), bf16[32,3,128,128]{3,2,1,0:T(8,128)(2,1)}, u32[]{:S(2)}, u32[]{:S(2)}) async-start(bf16[32,3,128,128]{3,2,1,0:T(8,128)(2,1)} %bitcast.58), calls=%async_computation.2 | async-start | bytes 6291456 | tf_op jit(solution)/shard_map/all_to_all | solution.py:60
  202.8 71.1 %all-to-all-done.2 = bf16[32,3,128,128]{3,2,1,0:T(8,128)(2,1)} async-done(((bf16[32,3,128,128]{3,2,1,0:T(8,128)(2,1)}), bf16[32,3,128,128]{3,2,1,0:T(8,128)(2,1)}, u32[]{:S(2)}, u32[]{:S(2)}) %all-to-all-start.2) | async-done | bytes 3145760 | tf_op jit(solution)/shard_map/all_to_all | solution.py:60
  273.9 2.8 gather_fusion.3
  276.7 2.6 select_convert_fusion
  (10 shorter events, 0.1 us)
Async XLA Ops:
  0.0 52.3 %copy-start = (bf16[7,2,128,128]{3,2,1,0:T(8,128)(2,1)S(1)}, bf16[7,2,128,128]{3,2,1,0:T(8,128)(2,1)}, u32[]{:S(2)}) copy-start(bf16[7,2,128,128]{3,2,1,0:T(8,128)(2,1)} %param.8) | copy-start | bytes 1376260
  0.0 19.4 %copy-start.2 = (bf16[7,2,128,128]{3,2,1,0:T(8,128)(2,1)S(1)}, bf16[7,2,128,128]{3,2,1,0:T(8,128)(2,1)}, u32[]{:S(2)}) copy-start(bf16[7,2,128,128]{3,2,1,0:T(8,128)(2,1)} %param.7) | copy-start | bytes 1376260
  3.1 42.3 %all-to-all-start = ((s32[32,1,3]{2,1,0:T(1,128)}), s32[32,1,3]{2,1,0:T(1,128)S(1)}, u32[]{:S(2)}, u32[]{:S(2)}) async-start(s32[32,1,3]{2,1,0:T(1,128)} %bitcast.10), calls=%async_computation | async-start | bytes 32768 | tf_op jit(solution)/shard_map/all_to_all | solution.py:47
  45.4 5.9 %copy-start.3 = (s32[7]{0:T(128)S(1)}, s32[7]{0:T(128)}, u32[]{:S(2)}) copy-start(s32[7]{0:T(128)} %param.11) | copy-start | bytes 88
  45.4 145.3 %all-to-all-start.1 = ((bf16[32,3,2,128,128]{4,3,2,1,0:T(8,128)(2,1)}), bf16[32,3,2,128,128]{4,3,2,1,0:T(8,128)(2,1)}, u32[]{:S(2)}, u32[]{:S(2)}) async-start(bf16[32,3,2,128,128]{4,3,2,1,0:T(8,128)(2,1)} %broadcast_select_fusion), calls=%async_computation.1 | async-start | bytes 12582912 | tf_op jit(solution)/shard_map/all_to_all | solution.py:46
  190.8 4.6 %copy-start.1 = (bf16[96,2,128,128]{3,2,1,0:T(8,128)(2,1)S(1)}, bf16[96,2,128,128]{3,2,1,0:T(8,128)(2,1)}, u32[]{:S(2)}) copy-start(bf16[96,2,128,128]{3,2,1,0:T(8,128)(2,1)} %gather_fusion.2) | copy-start | bytes 18874372
  198.9 75.0 %all-to-all-start.2 = ((bf16[32,3,128,128]{3,2,1,0:T(8,128)(2,1)}), bf16[32,3,128,128]{3,2,1,0:T(8,128)(2,1)}, u32[]{:S(2)}, u32[]{:S(2)}) async-start(bf16[32,3,128,128]{3,2,1,0:T(8,128)(2,1)} %bitcast.58), calls=%async_computation.2 | async-start | bytes 6291456 | tf_op jit(solution)/shard_map/all_to_all | solution.py:60
where the time goes:
time: 281 us; the launch traced here: 279 us
  waiting for transfers between devices  199 us (71%)
  local copies, waits for them, and re-layouts  33.3 us (12%)
  other arithmetic  25.1 us (9%)
  starting transfers between devices  16.9 us (6%)
  matrix products  4.66 us (2%)
    all_to_all x1, waiting for transfers between devices, body(): lax.all_to_all(outgoing, 'blk', split_axis=0, concat_axis=0, tiled=True)  128 us
    all_to_all x1, waiting for transfers between devices, body(): lax.all_to_all(products.reshape(senders, per_sender, extent, extent), 'bl...  71.1 us
    gather x2, local copies, waits for them, and re-layouts, body(): jnp.take(padded, source, axis=0)  16.6 us
    all_to_all x1, starting transfers between devices, body(): lax.all_to_all(wanted, 'blk', split_axis=0, concat_axis=0, tiled=True)  7.1 us
    select_n x2, other arithmetic, body(): jnp.take(padded, source, axis=0)  6.03 us
    gather x1, local copies, waits for them, and re-layouts, body(): operators = right_environment[clipped]  5.92 us
    all_to_all x1, starting transfers between devices, body(): lax.all_to_all(outgoing, 'blk', split_axis=0, concat_axis=0, tiled=True)  5.85 us
  transfers between devices with their start and end apart: 3, of which 2 were waited for; matrix products, arithmetic and copies ran while one was open for 17% of the time, Pallas kernels for 0%

commit v1 on v0

v1 whole, which is shorter than its diff:
```python
import jax
import jax.numpy as jnp
from jax import lax
from jax.sharding import PartitionSpec as P

PER_SECTOR = 8


def keep_below(limits, extent):
    return jnp.arange(extent, dtype=jnp.int32)[None, :] < limits[:, None]


def body(wavefunction, left_environment, right_environment, right_sector, left_dims, right_dims):
    blocks_here, extent, _ = wavefunction.shape
    sectors_here, terms_here = (left_environment.shape[0], left_environment.shape[1])
    right_all = lax.all_gather(right_environment, "blk", axis=0, tiled=True)
    dims_all = lax.all_gather(right_dims, "blk", axis=0, tiled=True)
    left_index = jnp.arange(blocks_here, dtype=jnp.int32) // PER_SECTOR
    row_keep = keep_below(left_dims[left_index], extent)
    masked = jnp.where(row_keep[:, :, None], wavefunction, jnp.zeros((), jnp.bfloat16))
    grouped = masked.reshape(sectors_here, PER_SECTOR, extent, extent)
    left_part = jnp.einsum(
        "atij,apjk->aptik", left_environment, grouped, preferred_element_type=jnp.float32
    )
    left_part = left_part.astype(jnp.bfloat16).reshape(blocks_here, terms_here, extent, extent)
    col_keep = keep_below(dims_all[right_sector], extent)
    left_part = jnp.where(col_keep[:, None, None, :], left_part, jnp.zeros((), jnp.bfloat16))
    operators = right_all[right_sector]
    products = jnp.einsum(
        "ntij,ntjk->nik", left_part, operators, preferred_element_type=jnp.float32
    )
    products = jnp.where(col_keep[:, None, :], products, 0.0).astype(jnp.bfloat16)
    summed = lax.psum_scatter(
        products, "term", scatter_dimension=1, tiled=True,
    ).astype(jnp.float32)
    rows_here = summed.shape[1]
    row_numbers = lax.axis_index("term") * rows_here + jnp.arange(rows_here, dtype=jnp.int32)
    keep_rows = row_numbers[None, :] < left_dims[left_index][:, None]
    return jnp.where(keep_rows[:, :, None], summed, 0.0).astype(jnp.bfloat16)


def solution(mesh):
    placed = (
        P(("groups", "blk"), None, None),
        P(("groups", "blk"), "term", None, None),
        P(("groups", "blk"), "term", None, None),
        P(("groups", "blk")),
        P(("groups", "blk")),
        P(("groups", "blk")),
    )
    return jax.shard_map(
        body,
        mesh=mesh,
        in_specs=placed,
        out_specs=P(("groups", "blk"), "term", None),
        check_vma=False,
    )
```

time: 281 us -> 139 us (0.49)
  waiting for transfers between devices: 199 us -> 50.2 us
  blocking collectives: 0 us -> 42.1 us
  other arithmetic: 25.1 us -> 7.76 us
  starting transfers between devices: 16.9 us -> 0.01 us
  local copies, waits for them, and re-layouts: 33.3 us -> 16.6 us
  between operations: 0.2 us -> 13.4 us
  matrix products: 4.66 us -> 8.04 us
    all_to_all x3 -> x0, waiting for transfers between devices: 199 us -> none  [the longest x1 128 us: body(): lax.all_to_all(outgoing, 'blk', split_axis=0, concat_axis=0, tiled=True)]
    all_gather x0 -> x1, waiting for transfers between devices: none -> 49.5 us  [body(): right_all = lax.all_gather(right_environment, 'blk', axis=0, tiled=True)]
    unnamed x0 -> x1, blocking collectives: none -> 42.1 us
    gather x6 -> x2, local copies, waits for them, and re-layouts: 27.3 us -> 8.85 us  [the longest x1 8.06 us: body(): operators = right_all[right_sector]]
    all_to_all x3 -> x0, starting transfers between devices: 16.9 us -> none  [the longest x1 7.1 us: body(): lax.all_to_all(wanted, 'blk', split_axis=0, concat_axis=0, tiled=True)]
    select_n x9 -> x1, other arithmetic: 14.6 us -> 0.01 us  [body(): col_keep = keep_below(dims_all[right_sector], extent)]
    reshape x0 -> x1, local copies, waits for them, and re-layouts: none -> 5.97 us  [body(): left_part.astype(jnp.bfloat16)]
  transfers between devices with their start and end apart: 3 -> 1, of which waited for: 2 -> 1; matrix products, arithmetic and copies ran while one was open for 17% -> 14% of each run, Pallas kernels for 0% -> 0%
where the time goes in v1:
time: 139 us; the launch traced here: 138 us
  waiting for transfers between devices  50.2 us (36%)
  blocking collectives  42.1 us (30%)
  local copies, waits for them, and re-layouts  16.6 us (12%)
  between operations  13.4 us (10%)
  matrix products  8.04 us (6%)
  other arithmetic  7.76 us (6%)
    all_gather x1, waiting for transfers between devices, body(): right_all = lax.all_gather(right_environment, 'blk', axis=0, tiled=True)  49.5 us
    unnamed x1, blocking collectives  42.1 us
    gather x1, local copies, waits for them, and re-layouts, body(): operators = right_all[right_sector]  8.06 us
    reshape x1, local copies, waits for them, and re-layouts, body(): left_part.astype(jnp.bfloat16)  5.97 us
    dot_general x1, matrix products, body(): jnp.einsum('ntij,ntjk->nik', left_part, operators, preferred_element_type...  5.05 us
    gather x1, other arithmetic, body(): keep_rows = row_numbers[None, :] < left_dims[left_index][:, None]  4.56 us
    select_n x1, other arithmetic, body(): jnp.where(row_keep[:, :, None], wavefunction, jnp.zeros((), jnp.bfloat16))  3.04 us
    dot_general x1, matrix products, body(): jnp.einsum('atij,apjk->aptik', left_environment, grouped, preferred_eleme...  3 us
  transfers between devices with their start and end apart: 1, of which 1 were waited for; matrix products, arithmetic and copies ran while one was open for 14% of the time, Pallas kernels for 0%

profile of v1, /device:TPU:1, one launch (start us, length us, event | category | flops | bytes accessed | tf_op | source)
XLA Modules:
  0.0 138.2 jit_solution(1098399864551915567)
XLA Ops:
  6.5 0.0 copy-start
  6.5 0.0 all-gather.2.cloned.1.call-start
  6.5 0.7 all-gather.2.cloned.1.call-update
  7.3 1.6 %fusion.10 = (s32[1]{0:T(128)}, s32[1]{0:T(128)}, s32[1]{0:T(128)}, s32[1]{0:T(128)}, s32[1]{0:T(128)}, /*index=5*/s32[1]{0:T(128)}, s32[1]{0:T(128)}) fusion(s32[7]{0:T(128)} %param.10), kind=kLoop, calls=%fused_computation.29 | loop fusion | bytes 56 | tf_op jit(solution)/shard_map/gather | solution.py:38
  8.9 4.6 %fusion.8 = s32[56]{0:T(128)S(1)} fusion(s32[]{:T(128)} %bitcast, s32[]{:T(128)} %bitcast.1, s32[]{:T(128)} %bitcast.2, s32[]{:T(128)} %bitcast.3, s32[]{:T(128)} %bitcast.4, s32[]{:T(128)} %bitcast.6, s32[]{:T(128)} %bitcast.5), kind=kLoop, calls=%fused_computation.27 | loop fusion | flops 1288 | bytes 252 | tf_op jit(solution)/shard_map/gather | solution.py:38
  13.4 0.1 iota_compare_fusion.1
  13.5 3.0 %broadcast_select_fusion = bf16[56,128,128]{2,1,0:T(8,128)(2,1)S(1)} fusion(bf16[56,128,128]{2,1,0:T(8,128)(2,1)} %param.6, pred[56,128]{1,0:T(8,128)(4,1)S(1)} %iota_compare_fusion.1), kind=kLoop, calls=%fused_computation.10 | loop fusion | flops 917504 | bytes 3677184 | tf_op jit(solution)/shard_map/jit(_where)/select_n | solution.py:20
  16.5 0.0 copy-done
  16.6 3.0 %convolution_convert_fusion = bf16[7,8,128,2,128]{4,2,3,1,0:T(8,128)(2,1)} fusion(bf16[7,8,128,128,1]{3,2,4,1,0:T(8,128)(2,1)S(1)} %bitcast.32, bf16[7,2,128,128]{3,2,1,0:T(8,128)(2,1)S(1)} %copy-done), kind=kOutput, calls=%fused_computation.8 | convolution fusion | flops 471597056 | bytes 5963776 | tf_op jit(solution)/shard_map/atij,apjk->aptik/dot_general | solution.py:22
  19.6 0.0 copy-start.1
  19.6 0.0 copy-start.2
  19.6 6.0 %copy.12 = bf16[56,2,128,128]{3,2,1,0:T(8,128)(2,1)} copy(bf16[56,2,128,128]{2,3,1,0:T(8,128)(2,1)} %bitcast.31) | data formatting | bytes 7340032 | tf_op jit(solution)/shard_map/reshape | solution.py:25
  25.5 0.0 copy-done.1
  25.5 0.2 dynamic-update-slice
  25.7 42.1 %all-reduce = s32[224]{0:T(256)S(1)} all-reduce(s32[224]{0:T(256)S(1)} %dynamic-update-slice), channel_id=1, replica_groups=mesh['groups'=1,'blk'=32,'term'=1] {'blk'}, use_global_device_ids=true, to_apply=%add | all-reduce | flops 224 | bytes 1792
  67.8 0.0 copy-done.2
  67.8 0.8 gather_fusion
  68.6 0.1 iota_compare_fusion
  68.7 49.5 %all-gather.2.cloned.1.call-done = bf16[224,2,128,128]{3,2,1,0:T(8,128)(2,1)} async-done(((bf16[7,2,128,128]{3,2,1,0:T(8,128)(2,1)}), bf16[224,2,128,128]{3,2,1,0:T(8,128)(2,1)}) %all-gather.2.cloned.1.call-update) | async-done | bytes 14680080 | tf_op jit(solution)/shard_map/all_gather | solution.py:16
  118.2 8.1 %gather_fusion.1 = bf16[56,2,128,128]{3,2,1,0:T(8,128)(2,1)} fusion(bf16[224,2,128,128]{3,2,1,0:T(8,128)(2,1)} %all-gather.2.cloned.1.call-done, s32[1024]{0:T(1024)S(1)} %pad_clamp_fusion), kind=kCustom, calls=%fused_computation.1 | custom fusion | bytes 7340256 | tf_op jit(solution)/shard_map/gather | solution.py:28
  126.3 5.0 %select_convert_fusion = bf16[56,128,128]{2,1,0:T(8,128)(2,1)} fusion(pred[56,128]{1,0:T(8,128)(4,1)S(1)} %iota_compare_fusion, pred[56,128]{1,0:T(8,128)(4,1)S(1)} %iota_compare_fusion.1, bf16[56,2,128,128]{3,2,1,0:T(8,128)(2,1)} %gather_fusion.1, bf16[56,2,128,128]{3,2,1,0:T(8,128)(2,1)} %copy.12), kind=kOutput, calls=%fused_computation.4 | convolution fusion | flops 476184576 | bytes 9189376 | tf_op jit(solution)/shard_map/ntij,ntjk->nik/dot_general | solution.py:29
  (3 shorter events, 0.0 us)
Async XLA Ops:
  6.5 10.0 %copy-start = (bf16[7,2,128,128]{3,2,1,0:T(8,128)(2,1)S(1)}, bf16[7,2,128,128]{3,2,1,0:T(8,128)(2,1)}, u32[]{:S(2)}) copy-start(bf16[7,2,128,128]{3,2,1,0:T(8,128)(2,1)} %param.7) | copy-start | bytes 1376260
  6.5 111.7 %all-gather.2.cloned.1.call-start = ((), (), s32[]{:S(2)}) async-start(), calls=%async_computation | async-start | bytes 15138816 | tf_op jit(solution)/shard_map/all_gather | solution.py:16
  19.6 6.0 %copy-start.1 = (s32[7]{0:T(128)S(1)}, s32[7]{0:T(128)}, u32[]{:S(2)}) copy-start(s32[7]{0:T(128)} %param.11) | copy-start | bytes 88
  19.6 48.2 %copy-start.2 = (s32[56]{0:T(128)S(1)}, s32[56]{0:T(128)}, u32[]{:S(2)}) copy-start(s32[56]{0:T(128)} %param.9) | copy-start | bytes 676
Sparse Core Ops, SparseCore 0:
  10.2 107.9 all-gather.1

commit v2 on v1

v2 whole, which is shorter than its diff:
```python
import functools

import jax
import jax.numpy as jnp
from jax import lax
from jax.experimental import pallas as pl
from jax.experimental.pallas import tpu as pltpu
from jax.sharding import PartitionSpec as P

PER_SECTOR = 8
VMEM_BYTES = 50 * 1024 * 1024
ROUTES = (("xzy", 2), ("yzx", 2), ("zxy", 1), ("zyx", 1))


def keep_below(limits, extent):
    return jnp.arange(extent, dtype=jnp.int32)[None, :] < limits[:, None]


def square_mask(operators, limits):
    keep = keep_below(limits, operators.shape[-1])
    keep = keep[:, None, :, None] & keep[:, None, None, :]
    return jnp.where(keep, operators, jnp.zeros((), operators.dtype))


def split_rows(rows):
    total = sum(weight for _, weight in ROUTES)
    parts, start, used = [], 0, 0
    for order, weight in ROUTES:
        used += weight
        stop = rows if used == total else rows * used // total // 16 * 16
        parts.append((order, start, stop - start))
        start = stop
    return parts


def kernel(devices, terms, psi_hbm, left_ref, right_ref, sector_ref, ldim_ref, rdim_ref, out_ref,
           gathered, psi, lmask, lpart, send_sem, recv_sem, psi_sem):
    sectors, _, extent, _ = right_ref.shape
    blocks = psi.shape[0]
    height = terms * extent
    depth = devices // 8
    me = lax.axis_index("blk")
    core, x, y, z = me % 2, (me // 2) % 2, (me // 4) % 2, me // 8

    def at(zz, yy, xx, cc):
        return zz * 8 + yy * 4 + xx * 2 + cc

    psi_copy = pltpu.make_async_copy(psi_hbm, psi, psi_sem)
    psi_copy.start()

    barrier = pltpu.get_barrier_semaphore()
    for peer in (at(z, y, x, 1 - core), at(z, y, 1 - x, core), at(z, 1 - y, x, core)):
        pl.semaphore_signal(barrier, inc=1, device_id={"blk": peer}, device_id_type=pl.DeviceIdType.MESH)

    @pl.when(z > 0)
    def _():
        pl.semaphore_signal(barrier, inc=1, device_id={"blk": me - 8}, device_id_type=pl.DeviceIdType.MESH)

    @pl.when(z < depth - 1)
    def _():
        pl.semaphore_signal(barrier, inc=1, device_id={"blk": me + 8}, device_id_type=pl.DeviceIdType.MESH)

    row_numbers = lax.broadcasted_iota(jnp.int32, (extent, extent), 0)
    col_numbers = lax.broadcasted_iota(jnp.int32, (extent, extent), 1)
    farthest = jnp.maximum(row_numbers, col_numbers)

    def mask_right(a, carry):
        keep = farthest < rdim_ref[a]
        for t in range(terms):
            gathered[me * sectors + a, pl.ds(t * extent, extent), :] = jnp.where(keep, right_ref[a, t].astype(jnp.float32), 0.0).astype(jnp.bfloat16)
        return carry

    lax.fori_loop(0, sectors, mask_right, 0)
    pl.semaphore_wait(barrier, 3 + jnp.where(z > 0, 1, 0) + jnp.where(z < depth - 1, 1, 0))

    parts = split_rows(height)

    def piece(p, origin):
        _, start, count = parts[p]
        return gathered.at[pl.ds(origin * sectors, sectors), pl.ds(start, count), :]

    sends = []

    def send(p, event, kind, origin, target, condition=None):
        def copy():
            return pltpu.make_async_remote_copy(
                src_ref=piece(p, origin), dst_ref=piece(p, origin),
                send_sem=send_sem.at[p, event, kind], recv_sem=recv_sem.at[p, origin],
                device_id={"blk": target}, device_id_type=pl.DeviceIdType.MESH)
        if condition is None:
            copy().start()
        else:
            pl.when(condition)(lambda: copy().start())
        sends.append((copy, condition))

    def wait_arrival(p, origin):
        pltpu.make_async_remote_copy(
            src_ref=piece(p, origin), dst_ref=piece(p, origin),
            send_sem=send_sem.at[p, 0, 0], recv_sem=recv_sem.at[p, origin],
            device_id={"blk": at(z, y, x, 1 - core)}, device_id_type=pl.DeviceIdType.MESH).wait_recv()

    def other(rank):
        low = z < depth // 2
        mine = jnp.where(low, z, depth - 1 - z)
        found = jnp.where(rank - 1 < mine, rank - 1, rank)
        return jnp.where(low, found, depth - 1 - found)

    def forward(p, event, origin, later, onward):
        if onward is not None:
            target_z, inside = onward
            send(p, event, 2, origin, at(target_z, y, x, core), inside)
        for dim in later:
            if dim == "z":
                send(p, event, 2, origin, me - 8, z > 0)
                send(p, event, 3, origin, me + 8, z < depth - 1)
            elif dim == "x":
                send(p, event, 0, origin, at(z, y, 1 - x, core))
            else:
                send(p, event, 1, origin, at(z, 1 - y, x, core))
        send(p, event, 4, origin, at(z, y, x, 1 - core))

    def left_sector(a):
        keep = farthest < ldim_ref[a]
        for t in range(terms):
            lmask[pl.ds(t * extent, extent), :] = jnp.where(
                keep, left_ref[a, t].astype(jnp.float32), 0.0).astype(jnp.bfloat16)

        def one(i, carry):
            k = a * PER_SECTOR + i
            both = jnp.dot(lmask[...], psi[k], preferred_element_type=jnp.float32)
            for t in range(terms):
                lpart[k, :, pl.ds(t * extent, extent)] = both[t * extent:(t + 1) * extent].astype(jnp.bfloat16)
            return carry

        lax.fori_loop(0, PER_SECTOR, one, 0, unroll=4)

    for p, (order, _, _) in enumerate(parts):
        forward(p, 0, me, order, None)
    psi_copy.wait()

    events = [(rank, dy, dx) for rank in range(depth) for dy in range(2) for dx in range(2)][1:]
    events.sort(key=lambda e: (sum(e), e))
    done = 0
    for number, (rank, dy, dx) in enumerate(events):
        origin_z = other(rank) if rank else z
        origin = at(origin_z, 1 - y if dy else y, 1 - x if dx else x, core)
        for p, (order, _, _) in enumerate(parts):
            differs = {"x": dx, "y": dy, "z": rank}
            arrived = max(i for i, dim in enumerate(order) if differs[dim])
            onward = None
            if order[arrived] == "z":
                below = origin_z < z
                onward = (jnp.where(below, z + 1, z - 1),
                          jnp.where(below, depth - 1 - z, z) > 0)
            wait_arrival(p, origin)
            forward(p, number + 1, origin, order[arrived + 1:], onward)
        if done < sectors:
            left_sector(done)
            done += 1
    for a in range(done, sectors):
        left_sector(a)

    for chip in range(devices // 2):
        for p in range(len(parts)):
            wait_arrival(p, chip * 2 + 1 - core)

    def right(k, carry):
        out_ref[k] = jnp.dot(lpart[k], gathered[sector_ref[k]], preferred_element_type=jnp.float32).astype(jnp.bfloat16)
        return carry

    lax.fori_loop(0, blocks, right, 0, unroll=4)

    for copy, condition in sends:
        if condition is None:
            copy().wait_send()
        else:
            pl.when(condition)(lambda copy=copy: copy().wait_send())


def fused(devices, wavefunction, left_environment, right_environment, right_sector, left_dims, right_dims):
    blocks, extent, _ = wavefunction.shape
    sectors, terms = left_environment.shape[:2]
    height = terms * extent
    parts = len(split_rows(height))
    vmem = pl.BlockSpec(memory_space=pltpu.VMEM)
    smem = pl.BlockSpec(memory_space=pltpu.SMEM)
    return pl.pallas_call(
        functools.partial(kernel, devices, terms),
        out_shape=jax.ShapeDtypeStruct((blocks, extent, extent), jnp.bfloat16),
        in_specs=[pl.BlockSpec(memory_space=pl.ANY), vmem, vmem, smem, smem, smem],
        out_specs=vmem,
        scratch_shapes=[
            pltpu.VMEM((devices * sectors, height, extent), jnp.bfloat16),
            pltpu.VMEM((blocks, extent, extent), jnp.bfloat16),
            pltpu.VMEM((height, extent), jnp.bfloat16),
            pltpu.VMEM((blocks, extent, height), jnp.bfloat16),
            pltpu.SemaphoreType.DMA((parts, devices // 2, 5)),
            pltpu.SemaphoreType.DMA((parts, devices)),
            pltpu.SemaphoreType.DMA,
        ],
        compiler_params=pltpu.CompilerParams(
            collective_id=0, has_side_effects=True, vmem_limit_bytes=VMEM_BYTES),
        cost_estimate=pl.CostEstimate(
            flops=4 * blocks * terms * extent ** 3, transcendentals=0,
            bytes_accessed=4 * blocks * extent * extent),
    )(wavefunction, left_environment, right_environment, right_sector, left_dims, right_dims)


def body(wavefunction, left_environment, right_environment, right_sector, left_dims, right_dims):
    devices = lax.axis_size("blk")
    blocks_here, extent, _ = wavefunction.shape
    sectors_here, terms_here = left_environment.shape[:2]
    needed = 2 * extent * extent * (terms_here * (devices + 1) * sectors_here + (3 + terms_here) * blocks_here)
    if lax.axis_size("term") == 1 and devices % 16 == 0 and needed < VMEM_BYTES * 3 // 4:
        return fused(devices, wavefunction, left_environment, right_environment, right_sector,
                     left_dims, right_dims)
    right_all = lax.all_gather(square_mask(right_environment, right_dims), "blk", axis=0, tiled=True)
    grouped = wavefunction.reshape(sectors_here, PER_SECTOR, extent, extent)
    left_part = jnp.einsum(
        "atij,apjk->aptik", square_mask(left_environment, left_dims), grouped,
        preferred_element_type=jnp.float32
    )
    left_part = left_part.astype(jnp.bfloat16).reshape(blocks_here, terms_here, extent, extent)
    products = jnp.einsum(
        "ntij,ntjk->nik", left_part, right_all[right_sector], preferred_element_type=jnp.float32
    ).astype(jnp.bfloat16)
    return lax.psum_scatter(products, "term", scatter_dimension=1, tiled=True)


def solution(mesh):
    placed = (
        P(("groups", "blk"), None, None),
        P(("groups", "blk"), "term", None, None),
        P(("groups", "blk"), "term", None, None),
        P(("groups", "blk")),
        P(("groups", "blk")),
        P(("groups", "blk")),
    )
    return jax.shard_map(
        body,
        mesh=mesh,
        in_specs=placed,
        out_specs=P(("groups", "blk"), "term", None),
        check_vma=False,
    )
```

time: 139 us -> 80.5 us (0.58)
  Pallas kernels: 0 us -> 75.1 us
  waiting for transfers between devices: 50.2 us -> 0 us
  blocking collectives: 42.1 us -> 0 us
  between operations: 13.4 us -> 0.01 us
  local copies, waits for them, and re-layouts: 16.6 us -> 5.23 us
  matrix products: 8.04 us -> 0 us
  other arithmetic: 7.76 us -> 0 us
    pallas_call x0 -> x1, Pallas kernels: none -> 75.1 us  [fused(): pl.pallas_call(functools.partial(kernel, devices, terms), out_shape=jax.S...]
    all_gather x1 -> x0, waiting for transfers between devices: 49.5 us -> none  [body(): right_all = lax.all_gather(right_environment, 'blk', axis=0, tiled=True)]
    unnamed x1 -> x0, blocking collectives: 42.1 us -> none
    gather x3 -> x0, local copies, waits for them, and re-layouts: 10.4 us -> none  [the longest x1 8.06 us: body(): operators = right_all[right_sector]]
    dot_general x2 -> x0, matrix products: 8.04 us -> none  [the longest x1 5.05 us: body(): jnp.einsum('ntij,ntjk->nik', left_part, operators, preferred_element_type...]
    reshape x1 -> x0, local copies, waits for them, and re-layouts: 5.97 us -> none  [body(): left_part.astype(jnp.bfloat16)]
    unnamed x8 -> x11, local copies, waits for them, and re-layouts: 0.22 us -> 5.23 us
    gather x2 -> x0, other arithmetic: 4.57 us -> none  [the longest x1 4.56 us: body(): keep_rows = row_numbers[None, :] < left_dims[left_index][:, None]]
  transfers between devices with their start and end apart: 1 -> 0, of which waited for: 1 -> 0; matrix products, arithmetic and copies ran while one was open for 14% -> 0% of each run, Pallas kernels for 0% -> 0%
where the time goes in v2:
time: 80.5 us; the launch traced here: 80.3 us
  Pallas kernels  75.1 us (93%)
  local copies, waits for them, and re-layouts  5.23 us (6%)
    pallas_call x1, Pallas kernels, fused(): pl.pallas_call(functools.partial(kernel, devices, terms), out_shape=jax.S...  75.1 us
    unnamed x11, local copies, waits for them, and re-layouts  5.23 us

profile of v2, /device:TPU:1, one launch (start us, length us, event | category | flops | bytes accessed | tf_op | source)
XLA Modules:
  0.0 80.3 jit_solution(12807466276186804910)
XLA Ops:
  0.0 0.0 copy-start
  0.0 1.0 %copy-done = bf16[7,2,128,128]{3,2,1,0:T(8,128)(2,1)S(1)} copy-done((bf16[7,2,128,128]{3,2,1,0:T(8,128)(2,1)S(1)}, bf16[7,2,128,128]{3,2,1,0:T(8,128)(2,1)}, u32[]{:S(2)}) %copy-start) | copy-done | bytes 458776
  1.0 0.0 copy-start.1
  1.0 1.0 %copy-done.1 = bf16[7,2,128,128]{3,2,1,0:T(8,128)(2,1)S(1)} copy-done((bf16[7,2,128,128]{3,2,1,0:T(8,128)(2,1)S(1)}, bf16[7,2,128,128]{3,2,1,0:T(8,128)(2,1)}, u32[]{:S(2)}) %copy-start.1) | copy-done | bytes 458776
  2.0 0.0 copy-start.2
  2.0 0.7 copy-done.2
  2.7 0.0 copy-start.3
  2.7 0.7 copy-done.3
  3.4 0.0 copy-start.4
  3.4 0.7 copy-done.4
  4.0 75.1 %shard_map.64 = bf16[56,128,128]{2,1,0:T(8,128)(2,1)S(1)} custom-call(bf16[56,128,128]{2,1,0:T(8,128)(2,1)} %psi_hbm.1, bf16[7,2,128,128]{3,2,1,0:T(8,128)(2,1)S(1)} %copy-done, bf16[7,2,128,128]{3,2,1,0:T(8,128)(2,1)S(1)} %copy-done.1, s32[56]{0:T(128)S(1)} %copy-done.2, s32[7]{0:T(128)S(1)} %copy-done.3, s32[7]{0:T(128)S(1)} %copy-done.4), custom_call_target="tpu_custom_call" | custom-call | flops 939524096 | bytes 3670016 | tf_op jit(solution)/shard_map/pallas_call | solution.py:187
  79.1 1.2 %copy.8 = bf16[56,128,128]{2,1,0:T(8,128)(2,1)} copy(bf16[56,128,128]{2,1,0:T(8,128)(2,1)S(1)} %shard_map.64) | data formatting | bytes 3670016
Async XLA Ops:
  0.0 1.0 %copy-start = (bf16[7,2,128,128]{3,2,1,0:T(8,128)(2,1)S(1)}, bf16[7,2,128,128]{3,2,1,0:T(8,128)(2,1)}, u32[]{:S(2)}) copy-start(bf16[7,2,128,128]{3,2,1,0:T(8,128)(2,1)} %left_ref.1) | copy-start | bytes 1376260
  1.0 1.0 %copy-start.1 = (bf16[7,2,128,128]{3,2,1,0:T(8,128)(2,1)S(1)}, bf16[7,2,128,128]{3,2,1,0:T(8,128)(2,1)}, u32[]{:S(2)}) copy-start(bf16[7,2,128,128]{3,2,1,0:T(8,128)(2,1)} %right_ref.1) | copy-start | bytes 1376260
  2.0 0.7 copy-start.2
  2.7 0.7 copy-start.3
  3.4 0.7 copy-start.4

commit v3 on v2

--- a/solution.py
+++ b/solution.py
@@ -9,7 +9,7 @@
 
 PER_SECTOR = 8
 VMEM_BYTES = 50 * 1024 * 1024
-ROUTES = (("xzy", 2), ("yzx", 2), ("zxy", 1), ("zyx", 1))
+ROUTES = (("zyx", 4), ("xzy", 3))
 
 
 def keep_below(limits, extent):
@@ -22,19 +22,20 @@
     return jnp.where(keep, operators, jnp.zeros((), operators.dtype))
 
 
-def split_rows(rows):
+def split_sectors(sectors):
     total = sum(weight for _, weight in ROUTES)
     parts, start, used = [], 0, 0
     for order, weight in ROUTES:
         used += weight
-        stop = rows if used == total else rows * used // total // 16 * 16
+        stop = sectors * used // total
         parts.append((order, start, stop - start))
         start = stop
     return parts
 
 
-def kernel(devices, terms, psi_hbm, left_ref, right_ref, sector_ref, ldim_ref, rdim_ref, out_ref,
-           gathered, psi, lmask, lpart, send_sem, recv_sem, psi_sem):
+def kernel(devices, terms, psi_hbm, left_hbm, right_hbm, sector_hbm, ldim_hbm, rdim_hbm, out_ref,
+           gathered, psi, left_ref, right_ref, sector_ref, ldim_ref, rdim_ref, lmask, lpart,
+           send_sem, recv_sem, load_sem):
     sectors, _, extent, _ = right_ref.shape
     blocks = psi.shape[0]
     height = terms * extent
@@ -45,8 +46,14 @@
     def at(zz, yy, xx, cc):
         return zz * 8 + yy * 4 + xx * 2 + cc
 
-    psi_copy = pltpu.make_async_copy(psi_hbm, psi, psi_sem)
-    psi_copy.start()
+    loads = [
+        pltpu.make_async_copy(source, target, load_sem.at[i])
+        for i, (source, target) in enumerate((
+            (rdim_hbm, rdim_ref), (right_hbm, right_ref), (left_hbm, left_ref),
+            (psi_hbm, psi), (ldim_hbm, ldim_ref), (sector_hbm, sector_ref)))
+    ]
+    for load in loads:
+        load.start()
 
     barrier = pltpu.get_barrier_semaphore()
     for peer in (at(z, y, x, 1 - core), at(z, y, 1 - x, core), at(z, 1 - y, x, core)):
@@ -63,6 +70,9 @@
     row_numbers = lax.broadcasted_iota(jnp.int32, (extent, extent), 0)
     col_numbers = lax.broadcasted_iota(jnp.int32, (extent, extent), 1)
     farthest = jnp.maximum(row_numbers, col_numbers)
+
+    for load in loads[:2]:
+        load.wait()
 
     def mask_right(a, carry):
         keep = farthest < rdim_ref[a]
@@ -70,14 +80,12 @@
             gathered[me * sectors + a, pl.ds(t * extent, extent), :] = jnp.where(keep, right_ref[a, t].astype(jnp.float32), 0.0).astype(jnp.bfloat16)
         return carry
 
-    lax.fori_loop(0, sectors, mask_right, 0)
-    pl.semaphore_wait(barrier, 3 + jnp.where(z > 0, 1, 0) + jnp.where(z < depth - 1, 1, 0))
-
-    parts = split_rows(height)
+
+    parts = split_sectors(sectors)
 
     def piece(p, origin):
         _, start, count = parts[p]
-        return gathered.at[pl.ds(origin * sectors, sectors), pl.ds(start, count), :]
+        return gathered.at[pl.ds(origin * sectors + start, count)]
 
     sends = []
 
@@ -134,9 +142,13 @@
 
         lax.fori_loop(0, PER_SECTOR, one, 0, unroll=4)
 
-    for p, (order, _, _) in enumerate(parts):
+    for p, (order, start, count) in enumerate(parts):
+        lax.fori_loop(start, start + count, mask_right, 0)
+        if p == 0:
+            pl.semaphore_wait(barrier, 3 + jnp.where(z > 0, 1, 0) + jnp.where(z < depth - 1, 1, 0))
         forward(p, 0, me, order, None)
-    psi_copy.wait()
+    for load in loads[2:]:
+        load.wait()
 
     events = [(rank, dy, dx) for rank in range(depth) for dy in range(2) for dx in range(2)][1:]
     events.sort(key=lambda e: (sum(e), e))
@@ -181,22 +193,25 @@
     blocks, extent, _ = wavefunction.shape
     sectors, terms = left_environment.shape[:2]
     height = terms * extent
-    parts = len(split_rows(height))
-    vmem = pl.BlockSpec(memory_space=pltpu.VMEM)
-    smem = pl.BlockSpec(memory_space=pltpu.SMEM)
+    parts = len(split_sectors(sectors))
     return pl.pallas_call(
         functools.partial(kernel, devices, terms),
         out_shape=jax.ShapeDtypeStruct((blocks, extent, extent), jnp.bfloat16),
-        in_specs=[pl.BlockSpec(memory_space=pl.ANY), vmem, vmem, smem, smem, smem],
-        out_specs=vmem,
+        in_specs=[pl.BlockSpec(memory_space=pl.ANY)] * 6,
+        out_specs=pl.BlockSpec(memory_space=pltpu.VMEM),
         scratch_shapes=[
             pltpu.VMEM((devices * sectors, height, extent), jnp.bfloat16),
             pltpu.VMEM((blocks, extent, extent), jnp.bfloat16),
+            pltpu.VMEM(left_environment.shape, jnp.bfloat16),
+            pltpu.VMEM(right_environment.shape, jnp.bfloat16),
+            pltpu.SMEM((blocks,), jnp.int32),
+            pltpu.SMEM((sectors,), jnp.int32),
+            pltpu.SMEM((sectors,), jnp.int32),
             pltpu.VMEM((height, extent), jnp.bfloat16),
             pltpu.VMEM((blocks, extent, height), jnp.bfloat16),
             pltpu.SemaphoreType.DMA((parts, devices // 2, 5)),
             pltpu.SemaphoreType.DMA((parts, devices)),
-            pltpu.SemaphoreType.DMA,
+            pltpu.SemaphoreType.DMA((6,)),
         ],
         compiler_params=pltpu.CompilerParams(
             collective_id=0, has_side_effects=True, vmem_limit_bytes=VMEM_BYTES),
@@ -211,7 +226,7 @@
     blocks_here, extent, _ = wavefunction.shape
     sectors_here, terms_here = left_environment.shape[:2]
     needed = 2 * extent * extent * (terms_here * (devices + 1) * sectors_here + (3 + terms_here) * blocks_here)
-    if lax.axis_size("term") == 1 and devices % 16 == 0 and needed < VMEM_BYTES * 3 // 4:
+    if lax.axis_size("term") == 1 and devices % 16 == 0 and sectors_here > 1 and needed < VMEM_BYTES * 3 // 4:
         return fused(devices, wavefunction, left_environment, right_environment, right_sector,
                      left_dims, right_dims)
     right_all = lax.all_gather(square_mask(right_environment, right_dims), "blk", axis=0, tiled=True)

time: 80.5 us -> 78.3 us (0.973)
  Pallas kernels: 75.1 us -> 72.8 us
    pallas_call x1, Pallas kernels: 75.1 us -> 72.8 us  [fused(): pl.pallas_call(functools.partial(kernel, devices, terms), out_shape=jax.S...]
where the time goes in v3:
time: 78.3 us; the launch traced here: 78.1 us
  Pallas kernels  72.8 us (93%)
  local copies, waits for them, and re-layouts  5.23 us (7%)
    pallas_call x1, Pallas kernels, fused(): pl.pallas_call(functools.partial(kernel, devices, terms), out_shape=jax.S...  72.8 us
    unnamed x11, local copies, waits for them, and re-layouts  5.23 us

profile of v3, /device:TPU:1, one launch (start us, length us, event | category | flops | bytes accessed | tf_op | source)
XLA Modules:
  0.0 78.1 jit_solution(9295865955468757676)
XLA Ops:
  0.0 0.0 copy-start
  0.0 1.0 %copy-done = bf16[7,2,128,128]{3,2,1,0:T(8,128)(2,1)S(1)} copy-done((bf16[7,2,128,128]{3,2,1,0:T(8,128)(2,1)S(1)}, bf16[7,2,128,128]{3,2,1,0:T(8,128)(2,1)}, u32[]{:S(2)}) %copy-start) | copy-done | bytes 458776
  1.0 0.0 copy-start.1
  1.0 1.0 %copy-done.1 = bf16[7,2,128,128]{3,2,1,0:T(8,128)(2,1)S(1)} copy-done((bf16[7,2,128,128]{3,2,1,0:T(8,128)(2,1)S(1)}, bf16[7,2,128,128]{3,2,1,0:T(8,128)(2,1)}, u32[]{:S(2)}) %copy-start.1) | copy-done | bytes 458776
  2.0 0.0 copy-start.2
  2.0 0.7 copy-done.2
  2.7 0.0 copy-start.3
  2.7 0.7 copy-done.3
  3.4 0.0 copy-start.4
  3.4 0.7 copy-done.4
  4.0 72.8 %shard_map.64 = bf16[56,128,128]{2,1,0:T(8,128)(2,1)S(1)} custom-call(bf16[56,128,128]{2,1,0:T(8,128)(2,1)} %psi_hbm.1, bf16[7,2,128,128]{3,2,1,0:T(8,128)(2,1)S(1)} %copy-done, bf16[7,2,128,128]{3,2,1,0:T(8,128)(2,1)S(1)} %copy-done.1, s32[56]{0:T(128)S(1)} %copy-done.2, s32[7]{0:T(128)S(1)} %copy-done.3, s32[7]{0:T(128)S(1)} %copy-done.4), custom_call_target="tpu_custom_call" | custom-call | flops 939524096 | bytes 3670016 | tf_op jit(solution)/shard_map/pallas_call | solution.py:197
  76.9 1.2 %copy.8 = bf16[56,128,128]{2,1,0:T(8,128)(2,1)} copy(bf16[56,128,128]{2,1,0:T(8,128)(2,1)S(1)} %shard_map.64) | data formatting | bytes 3670016
Async XLA Ops:
  0.0 1.0 %copy-start = (bf16[7,2,128,128]{3,2,1,0:T(8,128)(2,1)S(1)}, bf16[7,2,128,128]{3,2,1,0:T(8,128)(2,1)}, u32[]{:S(2)}) copy-start(bf16[7,2,128,128]{3,2,1,0:T(8,128)(2,1)} %left_hbm.1) | copy-start | bytes 1376260
  1.0 1.0 %copy-start.1 = (bf16[7,2,128,128]{3,2,1,0:T(8,128)(2,1)S(1)}, bf16[7,2,128,128]{3,2,1,0:T(8,128)(2,1)}, u32[]{:S(2)}) copy-start(bf16[7,2,128,128]{3,2,1,0:T(8,128)(2,1)} %right_hbm.1) | copy-start | bytes 1376260
  2.0 0.7 copy-start.2
  2.7 0.7 copy-start.3
  3.4 0.7 copy-start.4

commit v4 on v3

--- a/solution.py
+++ b/solution.py
@@ -151,7 +151,7 @@
         load.wait()
 
     events = [(rank, dy, dx) for rank in range(depth) for dy in range(2) for dx in range(2)][1:]
-    events.sort(key=lambda e: (sum(e), e))
+    events.sort(key=lambda e: (sum(e), -e[0], e))
     done = 0
     for number, (rank, dy, dx) in enumerate(events):
         origin_z = other(rank) if rank else z

time: 78.3 us -> 73.4 us (0.937)
  Pallas kernels: 72.8 us -> 67.9 us
    pallas_call x1, Pallas kernels: 72.8 us -> 67.9 us  [fused(): pl.pallas_call(functools.partial(kernel, devices, terms), out_shape=jax.S...]
where the time goes in v4:
time: 73.4 us; the launch traced here: 73.2 us
  Pallas kernels  67.9 us (93%)
  local copies, waits for them, and re-layouts  5.23 us (7%)
    pallas_call x1, Pallas kernels, fused(): pl.pallas_call(functools.partial(kernel, devices, terms), out_shape=jax.S...  67.9 us
    unnamed x11, local copies, waits for them, and re-layouts  5.23 us

profile of v4, /device:TPU:1, one launch (start us, length us, event | category | flops | bytes accessed | tf_op | source)
XLA Modules:
  0.0 73.2 jit_solution(6479309914283655449)
XLA Ops:
  0.0 0.0 copy-start
  0.0 1.0 %copy-done = bf16[7,2,128,128]{3,2,1,0:T(8,128)(2,1)S(1)} copy-done((bf16[7,2,128,128]{3,2,1,0:T(8,128)(2,1)S(1)}, bf16[7,2,128,128]{3,2,1,0:T(8,128)(2,1)}, u32[]{:S(2)}) %copy-start) | copy-done | bytes 458776
  1.0 0.0 copy-start.1
  1.0 1.0 %copy-done.1 = bf16[7,2,128,128]{3,2,1,0:T(8,128)(2,1)S(1)} copy-done((bf16[7,2,128,128]{3,2,1,0:T(8,128)(2,1)S(1)}, bf16[7,2,128,128]{3,2,1,0:T(8,128)(2,1)}, u32[]{:S(2)}) %copy-start.1) | copy-done | bytes 458776
  2.0 0.0 copy-start.2
  2.0 0.7 copy-done.2
  2.7 0.0 copy-start.3
  2.7 0.7 copy-done.3
  3.4 0.0 copy-start.4
  3.4 0.7 copy-done.4
  4.0 67.9 %shard_map.64 = bf16[56,128,128]{2,1,0:T(8,128)(2,1)S(1)} custom-call(bf16[56,128,128]{2,1,0:T(8,128)(2,1)} %psi_hbm.1, bf16[7,2,128,128]{3,2,1,0:T(8,128)(2,1)S(1)} %copy-done, bf16[7,2,128,128]{3,2,1,0:T(8,128)(2,1)S(1)} %copy-done.1, s32[56]{0:T(128)S(1)} %copy-done.2, s32[7]{0:T(128)S(1)} %copy-done.3, s32[7]{0:T(128)S(1)} %copy-done.4), custom_call_target="tpu_custom_call" | custom-call | flops 939524096 | bytes 3670016 | tf_op jit(solution)/shard_map/pallas_call | solution.py:197
  71.9 1.2 %copy.8 = bf16[56,128,128]{2,1,0:T(8,128)(2,1)} copy(bf16[56,128,128]{2,1,0:T(8,128)(2,1)S(1)} %shard_map.64) | data formatting | bytes 3670016
Async XLA Ops:
  0.0 1.0 %copy-start = (bf16[7,2,128,128]{3,2,1,0:T(8,128)(2,1)S(1)}, bf16[7,2,128,128]{3,2,1,0:T(8,128)(2,1)}, u32[]{:S(2)}) copy-start(bf16[7,2,128,128]{3,2,1,0:T(8,128)(2,1)} %left_hbm.1) | copy-start | bytes 1376260
  1.0 1.0 %copy-start.1 = (bf16[7,2,128,128]{3,2,1,0:T(8,128)(2,1)S(1)}, bf16[7,2,128,128]{3,2,1,0:T(8,128)(2,1)}, u32[]{:S(2)}) copy-start(bf16[7,2,128,128]{3,2,1,0:T(8,128)(2,1)} %right_hbm.1) | copy-start | bytes 1376260
  2.0 0.7 copy-start.2
  2.7 0.7 copy-start.3
  3.4 0.7 copy-start.4

commit v5 on v4

--- a/solution.py
+++ b/solution.py
@@ -140,7 +140,7 @@
                 lpart[k, :, pl.ds(t * extent, extent)] = both[t * extent:(t + 1) * extent].astype(jnp.bfloat16)
             return carry
 
-        lax.fori_loop(0, PER_SECTOR, one, 0, unroll=4)
+        lax.fori_loop(0, PER_SECTOR, one, 0, unroll=8)
 
     for p, (order, start, count) in enumerate(parts):
         lax.fori_loop(start, start + count, mask_right, 0)
@@ -180,7 +180,7 @@
         out_ref[k] = jnp.dot(lpart[k], gathered[sector_ref[k]], preferred_element_type=jnp.float32).astype(jnp.bfloat16)
         return carry
 
-    lax.fori_loop(0, blocks, right, 0, unroll=4)
+    lax.fori_loop(0, blocks, right, 0, unroll=8)
 
     for copy, condition in sends:
         if condition is None:

time: 73.4 us -> 72.3 us (0.985)
  Pallas kernels: 67.9 us -> 66.8 us
    pallas_call x1, Pallas kernels: 67.9 us -> 66.8 us  [fused(): pl.pallas_call(functools.partial(kernel, devices, terms), out_shape=jax.S...]
where the time goes in v5:
time: 72.3 us; the launch traced here: 72.1 us
  Pallas kernels  66.8 us (92%)
  local copies, waits for them, and re-layouts  5.23 us (7%)
    pallas_call x1, Pallas kernels, fused(): pl.pallas_call(functools.partial(kernel, devices, terms), out_shape=jax.S...  66.8 us
    unnamed x11, local copies, waits for them, and re-layouts  5.23 us

profile of v5, /device:TPU:1, one launch (start us, length us, event | category | flops | bytes accessed | tf_op | source)
XLA Modules:
  0.0 72.1 jit_solution(822379808775283783)
XLA Ops:
  0.0 0.0 copy-start
  0.0 1.0 %copy-done = bf16[7,2,128,128]{3,2,1,0:T(8,128)(2,1)S(1)} copy-done((bf16[7,2,128,128]{3,2,1,0:T(8,128)(2,1)S(1)}, bf16[7,2,128,128]{3,2,1,0:T(8,128)(2,1)}, u32[]{:S(2)}) %copy-start) | copy-done | bytes 458776
  1.0 0.0 copy-start.1
  1.0 1.0 %copy-done.1 = bf16[7,2,128,128]{3,2,1,0:T(8,128)(2,1)S(1)} copy-done((bf16[7,2,128,128]{3,2,1,0:T(8,128)(2,1)S(1)}, bf16[7,2,128,128]{3,2,1,0:T(8,128)(2,1)}, u32[]{:S(2)}) %copy-start.1) | copy-done | bytes 458776
  2.0 0.0 copy-start.2
  2.0 0.7 copy-done.2
  2.7 0.0 copy-start.3
  2.7 0.7 copy-done.3
  3.4 0.0 copy-start.4
  3.4 0.7 copy-done.4
  4.0 66.8 %shard_map.64 = bf16[56,128,128]{2,1,0:T(8,128)(2,1)S(1)} custom-call(bf16[56,128,128]{2,1,0:T(8,128)(2,1)} %psi_hbm.1, bf16[7,2,128,128]{3,2,1,0:T(8,128)(2,1)S(1)} %copy-done, bf16[7,2,128,128]{3,2,1,0:T(8,128)(2,1)S(1)} %copy-done.1, s32[56]{0:T(128)S(1)} %copy-done.2, s32[7]{0:T(128)S(1)} %copy-done.3, s32[7]{0:T(128)S(1)} %copy-done.4), custom_call_target="tpu_custom_call" | custom-call | flops 939524096 | bytes 3670016 | tf_op jit(solution)/shard_map/pallas_call | solution.py:197
  70.9 1.2 %copy.8 = bf16[56,128,128]{2,1,0:T(8,128)(2,1)} copy(bf16[56,128,128]{2,1,0:T(8,128)(2,1)S(1)} %shard_map.64) | data formatting | bytes 3670016
Async XLA Ops:
  0.0 1.0 %copy-start = (bf16[7,2,128,128]{3,2,1,0:T(8,128)(2,1)S(1)}, bf16[7,2,128,128]{3,2,1,0:T(8,128)(2,1)}, u32[]{:S(2)}) copy-start(bf16[7,2,128,128]{3,2,1,0:T(8,128)(2,1)} %left_hbm.1) | copy-start | bytes 1376260
  1.0 1.0 %copy-start.1 = (bf16[7,2,128,128]{3,2,1,0:T(8,128)(2,1)S(1)}, bf16[7,2,128,128]{3,2,1,0:T(8,128)(2,1)}, u32[]{:S(2)}) copy-start(bf16[7,2,128,128]{3,2,1,0:T(8,128)(2,1)} %right_hbm.1) | copy-start | bytes 1376260
  2.0 0.7 copy-start.2
  2.7 0.7 copy-start.3
  3.4 0.7 copy-start.4
